TPU v7x, 32 devices: a whole 2x2x4 slice. The times are simulated.
32 devices in a mesh: gy: 4 (over z), gz: 8 (over y, x, core).
Axes of the slice: x: 2, y: 2, z: 4, core: 2. Of those that a mesh axis runs over, the one named last changes fastest.
Arguments:
- fields: bfloat16 [1024, 16, 64, 64], P(None, 'gy', 'gz'), may hold values from -6 to 6
- spec_weight: float32 [32, 2, 64, 64], P('gz'), may hold values from -1.5 to 1.5
- skip_weight: bfloat16 [64, 64], replicated, may hold values from -0.75 to 0.75
- up_weight: bfloat16 [64, 256], replicated, may hold values from -0.75 to 0.75
- down_weight: bfloat16 [256, 64], replicated, may hold values from -0.375 to 0.375
- cotangent: bfloat16 [1024, 16, 64, 64], P(None, 'gy', 'gz'), may hold values from -6 to 6
Outputs:
- output: bfloat16 [1024, 16, 64, 64], P(None, 'gy', 'gz')
- grad_fields: bfloat16 [1024, 16, 64, 64], P(None, 'gy', 'gz')
- grad_spec: float32 [32, 2, 64, 64], P('gz')
- grad_skip: float32 [64, 64], replicated
- grad_up: float32 [64, 256], replicated
- grad_down: float32 [256, 64], replicated
All inputs are finite; a program needn't handle non-finite values.
Results may differ from a plain program's by a relative error of at most 0.0067.
Values sent between devices are 32-bit elements; how exact they have to be, the bound alone decides.
A program may use at most 192 MiB of HBM per device.

v0:
```python
import math

import jax
import jax.numpy as jnp
import numpy as np
from jax import lax
from jax.experimental import pallas as pl
from jax.experimental.pallas import tpu as pltpu
from jax.sharding import PartitionSpec as P

MODES = 32


CHUNK = 256
GELU_SCALE = math.sqrt(2.0 / math.pi)
GELU_CUBE = 0.044715


def fourier_tables(length_x, kept):
    position = np.arange(length_x)[:, None]
    wavenum = np.arange(kept)[None, :]
    phase = (position * wavenum % length_x) * (2.0 * np.pi / length_x)
    factor = 1.0 / math.sqrt(length_x)
    analysis = np.concatenate([np.cos(phase), -np.sin(phase)], axis=1) * factor
    doubled = np.where(wavenum == 0, 1.0, 2.0)
    synthesis = np.concatenate([np.cos(phase) * doubled, -np.sin(phase) * doubled], axis=1) * factor
    return (analysis.astype(np.float32), synthesis.astype(np.float32))


def split_table(table):
    high = table.astype(jnp.bfloat16)
    low = (table - high.astype(np.float32)).astype(jnp.bfloat16)
    return np.concatenate([high.T, high.T, low.T], axis=0)


def split_values(values):
    high = lax.reduce_precision(values, exponent_bits=8, mantissa_bits=7)
    low = (values - high).astype(jnp.bfloat16)
    high = high.astype(jnp.bfloat16)
    return [high, low, high]


def contract_lanes(left, right):
    return lax.dot_general(
        left, right, (((1,), (1,)), ((), ())), preferred_element_type=jnp.float32
    )


def dot(left, right):
    return jnp.dot(left, right, preferred_element_type=jnp.float32)


def gelu_and_slope(x):
    square = x * x
    t = jnp.tanh(x * (GELU_SCALE + (GELU_SCALE * GELU_CUBE) * square))
    half = 0.5 + 0.5 * t
    value = x * half
    slope = half + value * (1.0 - half) * (
        2.0 * GELU_SCALE + (6.0 * GELU_SCALE * GELU_CUBE) * square
    )
    return value, slope


def middle_kernel(
    u_ref, g_ref, coef_ref, table_ref, up_ref, up_t_ref, down_ref, down_t_ref,
    out_ref, pg_ref, both_ref, gup_ref, gdown_ref,
):
    @pl.when(pl.program_id(0) == 0)
    def _():
        gup_ref[...] = jnp.zeros_like(gup_ref)
        gdown_ref[...] = jnp.zeros_like(gdown_ref)

    kept2 = table_ref.shape[0] // 3
    for p in range(u_ref.shape[0]):
        both = 0.0
        gup = 0.0
        gdown = 0.0
        for j in range(u_ref.shape[2] // CHUNK):
            cols = pl.ds(j * CHUNK, CHUNK)
            u = u_ref[p, :, cols]
            g = g_ref[p, :, cols]
            table = table_ref[:, cols]
            pre = dot(coef_ref[p], jnp.concatenate([table, u], axis=0))
            act, act_slope = gelu_and_slope(pre)
            act = act.astype(jnp.bfloat16)
            hidden, hidden_slope = gelu_and_slope(dot(up_t_ref[...], act))
            hidden = hidden.astype(jnp.bfloat16)
            out_ref[p, :, cols] = dot(down_t_ref[...], hidden).astype(jnp.bfloat16)
            hidden_grad = (dot(down_ref[...], g) * hidden_slope).astype(jnp.bfloat16)
            pg = (dot(up_ref[...], hidden_grad) * act_slope).astype(jnp.bfloat16)
            pg_ref[p, :, cols] = pg
            both += contract_lanes(pg, jnp.concatenate([table[:kept2], u], axis=0))
            gdown += contract_lanes(hidden, g)
            gup += contract_lanes(hidden_grad, act)
        both_ref[p] = both
        gup_ref[...] += gup
        gdown_ref[...] += gdown


def final_kernel(pg_ref, coef_ref, table_ref, out_ref):
    for p in range(pg_ref.shape[0]):
        rows = jnp.concatenate([table_ref[...], pg_ref[p]], axis=0)
        out_ref[p] = dot(coef_ref[p], rows).astype(jnp.bfloat16)


def per_pencil(step, rows, cols):
    return pl.BlockSpec((step, rows, cols), lambda i: (i, 0, 0))


def whole(*shape):
    return pl.BlockSpec(shape, lambda i: (0,) * len(shape))


def mixer_of(weight):
    real_part = weight[:, 0]
    imag_part = weight[:, 1]
    upper = jnp.concatenate([real_part, imag_part], axis=2)
    lower = jnp.concatenate([-imag_part, real_part], axis=2)
    return jnp.concatenate([upper, lower], axis=1)


def weight_grad(moment, channels):
    real_grad = moment[:, :channels, :channels] + moment[:, channels:, channels:]
    imag_grad = moment[:, :channels, channels:] - moment[:, channels:, :channels]
    return jnp.stack([real_grad, imag_grad], axis=1)


def mix_modes(spectra, mixer4, channels):
    halves, kept, width = spectra.shape
    pencils = width // channels
    mixed = jnp.einsum(
        "rkpc,krcsd->skpd",
        spectra.reshape(halves, kept, pencils, channels),
        mixer4,
        precision=lax.Precision.HIGHEST,
    )
    return mixed.reshape(halves, kept, width)


def unmix_modes(grads, mixer4, channels):
    halves, kept, width = grads.shape
    pencils = width // channels
    back = jnp.einsum(
        "skpd,krcsd->rkpc",
        grads.reshape(halves, kept, pencils, channels),
        mixer4,
        precision=lax.Precision.HIGHEST,
    )
    return back.reshape(halves, kept, width)


def mode_moment(spectra, grads, channels):
    halves, kept, width = spectra.shape
    pencils = width // channels
    moment = jnp.einsum(
        "rkpc,skpd->krcsd",
        spectra.reshape(halves, kept, pencils, channels),
        grads.reshape(halves, kept, pencils, channels),
        precision=lax.Precision.HIGHEST,
    )
    return moment.reshape(kept, 2 * channels, 2 * channels)


def local(fields, spec_weight, skip_weight, up_weight, down_weight, cotangent):
    length_x, count_y, count_z, channels = fields.shape
    hidden_units = up_weight.shape[1]
    pencils = count_y * count_z
    kept2 = 2 * MODES
    depth = 3 * kept2 + channels
    analysis, synthesis = fourier_tables(length_x, MODES)
    gathered = lax.all_gather(spec_weight, "gz", axis=0, tiled=True)
    u = fields.transpose(1, 2, 3, 0).reshape(pencils, channels, length_x)
    g = cotangent.transpose(1, 2, 3, 0).reshape(pencils, channels, length_x)
    spectra = lax.dot_general(
        jnp.asarray(analysis.astype(jnp.bfloat16)),
        u.reshape(pencils * channels, length_x),
        (((0,), (1,)), ((), ())),
        preferred_element_type=jnp.float32,
    ).reshape(2, MODES, pencils * channels)
    mixer4 = mixer_of(gathered).reshape(MODES, 2, channels, 2, channels)

    def by_pencil(stacked):
        return stacked.reshape(kept2, pencils, channels).transpose(1, 2, 0)

    def with_weight(stacked, weight):
        repeated = jnp.broadcast_to(weight[None], (pencils, channels, channels))
        return jnp.concatenate(split_values(by_pencil(stacked)) + [repeated], axis=2)

    coef = with_weight(mix_modes(spectra, mixer4, channels), skip_weight.T)
    step = 2 if pencils % 2 == 0 else 1
    result, pre_grad, both, gup, gdown = pl.pallas_call(
        middle_kernel,
        grid=(pencils // step,),
        in_specs=[
            per_pencil(step, channels, length_x),
            per_pencil(step, channels, length_x),
            per_pencil(step, channels, depth),
            whole(3 * kept2, length_x),
            whole(channels, hidden_units),
            whole(hidden_units, channels),
            whole(hidden_units, channels),
            whole(channels, hidden_units),
        ],
        out_specs=[
            per_pencil(step, channels, length_x),
            per_pencil(step, channels, length_x),
            per_pencil(step, channels, kept2 + channels),
            whole(hidden_units, channels),
            whole(hidden_units, channels),
        ],
        out_shape=[
            jax.ShapeDtypeStruct((pencils, channels, length_x), jnp.bfloat16),
            jax.ShapeDtypeStruct((pencils, channels, length_x), jnp.bfloat16),
            jax.ShapeDtypeStruct((pencils, channels, kept2 + channels), jnp.float32),
            jax.ShapeDtypeStruct((hidden_units, channels), jnp.float32),
            jax.ShapeDtypeStruct((hidden_units, channels), jnp.float32),
        ],
        compiler_params=pltpu.CompilerParams(vmem_limit_bytes=40 * 1024 * 1024),
        name="middle",
    )(
        u, g, coef, jnp.asarray(split_table(synthesis)),
        up_weight, up_weight.T, down_weight, down_weight.T,
    )
    gskip = jnp.sum(both[:, :, kept2:], axis=0).T
    coeff_grads = both[:, :, :kept2].transpose(2, 0, 1).reshape(2, MODES, pencils * channels)
    moment = mode_moment(spectra, coeff_grads, channels)
    owned_share = lax.psum_scatter(
        weight_grad(moment, channels), "gz", scatter_dimension=0, tiled=True
    )
    spec_total = lax.psum(owned_share, "gy")
    packed = lax.psum(jnp.concatenate([gdown, gup, gskip], axis=0), ("gy", "gz"))
    back = with_weight(unmix_modes(coeff_grads, mixer4, channels), skip_weight)
    grad_fields = pl.pallas_call(
        final_kernel,
        grid=(pencils // step,),
        in_specs=[
            per_pencil(step, channels, length_x),
            per_pencil(step, channels, depth),
            whole(3 * kept2, length_x),
        ],
        out_specs=per_pencil(step, channels, length_x),
        out_shape=jax.ShapeDtypeStruct((pencils, channels, length_x), jnp.bfloat16),
        compiler_params=pltpu.CompilerParams(vmem_limit_bytes=40 * 1024 * 1024),
        name="final",
    )(pre_grad, back, jnp.asarray(split_table(analysis)))
    all_pencils = pencils * lax.axis_size("gy") * lax.axis_size("gz")
    cell_scale = 1.0 / math.sqrt(length_x * all_pencils)
    pencil_scale = 1.0 / math.sqrt(all_pencils)

    def to_grid(rows):
        return rows.reshape(count_y, count_z, channels, length_x).transpose(3, 0, 1, 2)

    return (
        to_grid(result),
        to_grid(grad_fields),
        spec_total * pencil_scale,
        packed[2 * hidden_units :] * cell_scale,
        packed[hidden_units : 2 * hidden_units].T * cell_scale,
        packed[:hidden_units] * cell_scale,
    )


def solution(mesh):
    placed = (
        P(None, "gy", "gz", None),
        P("gz", None, None, None),
        P(),
        P(),
        P(),
        P(None, "gy", "gz", None),
    )
    return jax.shard_map(
        local,
        mesh=mesh,
        in_specs=placed,
        out_specs=(
            P(None, "gy", "gz", None),
            P(None, "gy", "gz", None),
            P("gz", None, None, None),
            P(),
            P(),
            P(),
        ),
        check_vma=False,
    )
```

profile of v0, /device:TPU:0, one launch (start us, length us, event | category | flops | bytes accessed | tf_op | source)
XLA Modules:
  0.0 397.5 jit_solution(17746686050281291559)
XLA Ops:
  7.2 0.7 all-gather.2.cloned.1.call-update
  8.0 0.8 copy.53
  8.8 0.9 copy.54
  9.6 0.9 copy.55.down_ref
  10.5 1.2 dynamic-slice
  12.4 4.4 %convolution_bitcast_fusion = f32[2,32,32,64,1]{3,1,2,0,4:T(8,128)S(1)} fusion(bf16[2,32,1024,1]{2,1,3,0:T(8,128)(2,1)} %constant.24, bf16[32,64,1024,1]{2,1,0,3:T(8,128)(2,1)} %bitcast.69), kind=kOutput, calls=%fused_computation.10 | convolution fusion | flops 268435456 | bytes 4849664 | tf_op jit(solution)/shard_map/dot_general | solution.py:174
  16.8 23.7 %all-gather.2.cloned.1.call-done = f32[32,2,64,64]{3,2,1,0:T(8,128)} async-done(((f32[4,2,64,64]{3,2,1,0:T(8,128)}), f32[32,2,64,64]{3,2,1,0:T(8,128)}) %all-gather.2.cloned.1.call-update) | async-done | bytes 1048592 | tf_op jit(solution)/shard_map/all_gather | solution.py:171
  40.5 1.8 slice_bitcast_fusion
  42.4 0.4 copy-done.7
  42.7 0.1 fusion.20
  42.9 1.9 maximum_maximum_fusion
  44.8 5.6 %reshape.37 = f32[32,2,64,2,64]{4,3,2,1,0:T(2,128)} reshape(f32[32,128,128]{2,1,0:T(8,128)} %maximum_maximum_fusion) | data formatting | bytes 4194304 | tf_op jit(solution)/shard_map/reshape | solution.py:180
  50.4 5.1 %fusion.4 = f32[2,32,32,64]{3,2,0,1:T(8,128)S(1)} fusion(f32[32,2,64,2,64]{4,3,2,1,0:T(2,128)} %reshape.37, f32[2,32,32,64,1]{3,1,2,0,4:T(8,128)S(1)} %convolution_bitcast_fusion), kind=kOutput, calls=%fused_computation.11 | convolution fusion | flops 201326592 | bytes 3145728 | tf_op jit(solution)/shard_map/rkpc,krcsd->skpd/dot_general | solution.py:131
  55.6 0.6 copy.52
  56.2 0.3 fusion.10
  56.5 0.1 broadcast_in_dim.4
  56.7 0.7 pad_maximum_fusion.1.coef_ref
  57.3 1.1 copy-done
  58.4 0.1 copy-done.4
  58.5 83.6 %middle.1 = (bf16[32,64,1024]{2,1,0:T(8,128)(2,1)}, bf16[32,64,1024]{2,1,0:T(8,128)(2,1)S(1)}, f32[32,64,128]{2,1,0:T(8,128)S(1)}, f32[256,64]{1,0:T(8,128)S(1)}, f32[256,64]{1,0:T(8,128)S(1)}) custom-call(bf16[32,64,1024]{2,1,0:T(8,128)(2,1)S(1)} %bitcast.70, bf16[32,64,1024]{2,1,0:T(8,128)(2,1)} %bitcast.76, ...), custom_call_target="tpu_custom_call" | custom-call | tf_op jit(solution)/shard_map/middle/pallas_call | solution.py:191
  142.2 2.0 copy-done.1
  144.1 0.3 slice_reduce_fusion
  144.5 0.9 copy.56
  145.4 7.7 %fusion.7 = f32[2,32,32,64]{3,2,0,1:T(8,128)S(1)} fusion(f32[32,2,64,2,64]{4,3,2,1,0:T(2,128)} %reshape.37, f32[2,32,32,64,1]{3,2,1,0,4:T(8,128)S(1)} %bitcast.73), kind=kOutput, calls=%fused_computation.12 | convolution fusion | flops 201326592 | bytes 3145728 | tf_op jit(solution)/shard_map/skpd,krcsd->rkpc/dot_general | solution.py:143
  153.1 6.1 %fusion.14 = f32[32,2,64,2,64]{4,2,3,1,0:T(8,128)} fusion(f32[2,32,32,64,1]{3,1,2,0,4:T(8,128)S(1)} %convolution_bitcast_fusion, f32[2,32,32,64,1]{3,2,1,0,4:T(8,128)S(1)} %bitcast.74), kind=kOutput, calls=%fused_computation.23 | convolution fusion | flops 201326592 | bytes 3145728 | tf_op jit(solution)/shard_map/rkpc,skpd->krcsd/dot_general | solution.py:155
  159.3 0.8 pad_maximum_fusion.3
  160.2 8.0 %copy.63 = f32[32,2,64,2,64]{4,3,2,1,0:T(2,128)} copy(f32[32,2,64,2,64]{4,2,3,1,0:T(8,128)} %fusion.14) | data formatting | bytes 4194304 | tf_op jit(solution)/shard_map/rkpc,skpd->krcsd/dot_general | solution.py:155
  168.2 4.3 %reshape.40 = f32[32,128,128]{2,1,0:T(8,128)S(1)} reshape(f32[32,2,64,2,64]{4,3,2,1,0:T(2,128)} %copy.63) | data formatting | bytes 4194304 | tf_op jit(solution)/shard_map/reshape | solution.py:161
  172.5 0.6 fusion.13
  173.1 1.5 pad_maximum_fusion
  174.7 0.6 copy.60
  175.4 0.3 fusion.11
  175.7 0.3 copy-done.8
  176.1 0.1 broadcast_in_dim.5
  176.2 0.7 pad_maximum_fusion.2.coef_ref
  176.9 0.8 copy-done.2
  177.6 0.1 copy-done.3
  177.8 8.3 %final.1 = bf16[32,64,1024]{2,1,0:T(8,128)(2,1)} custom-call(bf16[32,64,1024]{2,1,0:T(8,128)(2,1)S(1)} %copy-done.2, bf16[32,64,256]{2,1,0:T(8,128)(2,1)S(1)} %pad_maximum_fusion.2.coef_ref, bf16[192,1024]{1,0:T(8,128)(2,1)S(1)} %copy-done.3), custom_call_target="tpu_custom_call" | custom-call | tf_op jit(solution)/shard_map/final/pallas_call | solution.py:233
  186.1 99.8 %all-reduce.7.cloned.1.call-done = f32[576,64]{1,0:T(8,128)} async-done(((f32[576,64]{1,0:T(8,128)}), f32[576,64]{1,0:T(8,128)}) %all-reduce.7.cloned.1.call-update) | async-done | bytes 147472 | tf_op jit(solution)/shard_map/psum | solution.py:231
  285.9 1.0 slice_multiply_fusion
  286.9 0.7 copy.66
  287.6 0.7 copy.67
  288.3 63.6 %all-reduce.9.cloned.1.call-done = f32[32,2,64,64]{3,2,0,1:T(8,128)} async-done(((f32[32,2,64,64]{3,2,0,1:T(8,128)}), f32[32,2,64,64]{3,2,0,1:T(8,128)}) %all-reduce.9.cloned.1.call-update) | async-done | bytes 1048592
  351.8 1.7 constant_dynamic-slice_fusion
  353.5 1.4 slice_multiply_fusion.2
  354.9 34.3 %all-reduce.5.cloned.1.call-done = f32[4,2,64,64]{3,2,0,1:T(8,128)} async-done(((f32[4,2,64,64]{3,2,0,1:T(8,128)}), f32[4,2,64,64]{3,2,0,1:T(8,128)}) %all-reduce.5.cloned.1.call-update) | async-done | bytes 131088 | tf_op jit(solution)/shard_map/psum | solution.py:230
  389.3 1.0 broadcast_multiply_fusion
  390.2 0.7 copy.65
  (21 shorter events, 0.5 us)
Async XLA Ops:
  7.2 33.4 %all-gather.2.cloned.1.call-start = ((), (), s32[]{:S(2)}) async-start(), calls=%async_computation | async-start | bytes 2359296 | tf_op jit(solution)/shard_map/all_gather | solution.py:171
  7.9 278.0 %all-reduce.7.cloned.1.call-start = ((), (), s32[]{:S(2)}) async-start(), calls=%async_computation.2 | async-start | bytes 589824 | tf_op jit(solution)/shard_map/psum | solution.py:231
  40.5 2.2 copy-start.7
  56.2 2.2 copy-start
  56.5 2.0 copy-start.4
  56.5 2.0 copy-start.5
  56.5 2.0 copy-start.6
  142.2 2.0 copy-start.1
  160.1 191.7 %all-reduce.9.cloned.1.call-start = ((), (), s32[]{:S(2)}) async-start(), calls=%async_computation.3 | async-start | bytes 4194304
  175.3 0.7 copy-start.8
  175.4 213.9 %all-reduce.5.cloned.1.call-start = ((), (), s32[]{:S(2)}) async-start(), calls=%async_computation.1 | async-start | bytes 524288 | tf_op jit(solution)/shard_map/psum | solution.py:230
  175.4 2.2 copy-start.2
  175.7 2.1 copy-start.3
Sparse Core Ops, SparseCore 0:
  9.9 30.5 all-gather.1
  160.2 125.6 all-reduce.6
  289.5 62.3 all-reduce.8
  354.7 34.4 all-reduce.4
where the time goes:
time: 398 us; the launch traced here: 397 us
  waiting for transfers between devices  222 us (56%)
  Pallas kernels  91.9 us (23%)
  local copies, waits for them, and re-layouts  34.8 us (9%)
  matrix products  23.3 us (6%)
  between operations  14.6 us (4%)
  other arithmetic  10.5 us (3%)
    psum x1, waiting for transfers between devices, local(): lax.psum(jnp.concatenate([gdown, gup, gskip], axis=0), ('gy', 'gz'))  99.8 us
    pallas_call x1, Pallas kernels, local(): pl.pallas_call(middle_kernel, grid=(pencils // step,), in_specs=[per_penc...  83.6 us
    unnamed x5, waiting for transfers between devices  64.3 us
    psum x1, waiting for transfers between devices, local(): spec_total = lax.psum(owned_share, 'gy')  34.3 us
    all_gather x1, waiting for transfers between devices, local(): gathered = lax.all_gather(spec_weight, 'gz', axis=0, tiled=True)  23.7 us
    unnamed x25, local copies, waits for them, and re-layouts  11.6 us
    pallas_call x1, Pallas kernels, local(): pl.pallas_call(final_kernel, grid=(pencils // step,), in_specs=[per_penci...  8.33 us
    dot_general x1, local copies, waits for them, and re-layouts, mode_moment(): jnp.einsum('rkpc,skpd->krcsd', spectra.reshape(halves, kept, pencils, cha...  8.04 us
  transfers between devices with their start and end apart: 4, of which 4 were waited for; matrix products, arithmetic and copies ran while one was open for 7% of the time, Pallas kernels for 2%

commit v1 on v0

--- a/solution.py
+++ b/solution.py
@@ -224,11 +224,16 @@
     gskip = jnp.sum(both[:, :, kept2:], axis=0).T
     coeff_grads = both[:, :, :kept2].transpose(2, 0, 1).reshape(2, MODES, pencils * channels)
     moment = mode_moment(spectra, coeff_grads, channels)
-    owned_share = lax.psum_scatter(
-        weight_grad(moment, channels), "gz", scatter_dimension=0, tiled=True
-    )
-    spec_total = lax.psum(owned_share, "gy")
-    packed = lax.psum(jnp.concatenate([gdown, gup, gskip], axis=0), ("gy", "gz"))
+    owners = lax.axis_size("gz")
+    spec_part = weight_grad(moment, channels).reshape(owners, -1, 128)
+    packed_part = jnp.concatenate([gdown, gup, gskip], axis=0).reshape(owners, -1, 128)
+    spec_rows = spec_part.shape[1]
+    shares = lax.all_to_all(
+        jnp.concatenate([spec_part, packed_part], axis=1), "gz", 0, 0, tiled=True
+    )
+    owned = jnp.sum(lax.all_gather(jnp.sum(shares, axis=0), "gy", axis=0), axis=0)
+    spec_total = owned[:spec_rows].reshape(spec_weight.shape)
+    packed = lax.all_gather(owned[spec_rows:], "gz", axis=0).reshape(-1, channels)
     back = with_weight(unmix_modes(coeff_grads, mixer4, channels), skip_weight)
     grad_fields = pl.pallas_call(
         final_kernel,

time: 398 us -> 224 us (0.56)
  waiting for transfers between devices: 222 us -> 26.3 us
  blocking collectives: 0 us -> 27 us
  local copies, waits for them, and re-layouts: 34.8 us -> 30.2 us
    psum x2 -> x0, waiting for transfers between devices: 134 us -> none  [the longest x1 99.8 us: local(): lax.psum(jnp.concatenate([gdown, gup, gskip], axis=0), ('gy', 'gz'))]
    unnamed x5 -> x1, waiting for transfers between devices: 64.3 us -> 0.68 us
    all_gather x0 -> x2, blocking collectives: none -> 27 us  [the longest x1 17.5 us: local(): lax.all_gather(jnp.sum(shares, axis=0), 'gy', axis=0)]
    unnamed x25 -> x24, local copies, waits for them, and re-layouts: 11.6 us -> 8.04 us
  transfers between devices with their start and end apart: 4 -> 2, of which waited for: 4 -> 1; matrix products, arithmetic and copies ran while one was open for 7% -> 7% of each run, Pallas kernels for 2% -> 4%
where the time goes in v1:
time: 224 us
  Pallas kernels  92 us (41%)
  local copies, waits for them, and re-layouts  30.2 us (13%)
  blocking collectives  27 us (12%)
  waiting for transfers between devices  26.3 us (12%)
  matrix products  21.4 us (10%)
  between operations  14.3 us (6%)
  other arithmetic  8.67 us (4%)
  starting transfers between devices  3.6 us (2%)
    pallas_call x1, Pallas kernels, local(): pl.pallas_call(middle_kernel, grid=(pencils // step,), in_specs=[per_penc...  83.6 us
    all_gather x1, waiting for transfers between devices, local(): gathered = lax.all_gather(spec_weight, 'gz', axis=0, tiled=True)  25.7 us
    all_gather x1, blocking collectives, local(): lax.all_gather(jnp.sum(shares, axis=0), 'gy', axis=0)  17.5 us
    all_gather x1, blocking collectives, local(): lax.all_gather(owned[spec_rows:], 'gz', axis=0).reshape(-1, channels)  9.56 us
    pallas_call x1, Pallas kernels, local(): pl.pallas_call(final_kernel, grid=(pencils // step,), in_specs=[per_penci...  8.33 us
    unnamed x24, local copies, waits for them, and re-layouts  8.04 us
    dot_general x1, matrix products, unmix_modes(): jnp.einsum('skpd,krcsd->rkpc', grads.reshape(halves, kept, pencils, chann...  7.74 us
    dot_general x1, local copies, waits for them, and re-layouts, mode_moment(): jnp.einsum('rkpc,skpd->krcsd', spectra.reshape(halves, kept, pencils, cha...  5.8 us
  transfers between devices with their start and end apart: 2, of which 1 were waited for; matrix products, arithmetic and copies ran while one was open for 7% of the time, Pallas kernels for 4%

profile of v1, /device:TPU:0, one launch (start us, length us, event | category | flops | bytes accessed | tf_op | source)
XLA Modules:
  0.0 223.6 jit_solution(4251919577219319019)
XLA Ops:
  7.2 0.7 all-gather.6.cloned.1.call-update
  7.9 0.8 copy.50
  8.7 0.9 copy.51
  9.6 0.9 copy.52.down_ref
  10.5 4.4 %convolution_bitcast_fusion = f32[2,32,32,64,1]{3,1,2,0,4:T(8,128)S(1)} fusion(bf16[2,32,1024,1]{2,1,3,0:T(8,128)(2,1)} %constant.20, bf16[32,64,1024,1]{2,1,0,3:T(8,128)(2,1)} %bitcast.68), kind=kOutput, calls=%fused_computation.10 | convolution fusion | flops 268435456 | bytes 4849664 | tf_op jit(solution)/shard_map/dot_general | solution.py:174
  14.9 25.7 %all-gather.6.cloned.1.call-done = f32[32,2,64,64]{3,2,1,0:T(8,128)} async-done(((f32[4,2,64,64]{3,2,1,0:T(8,128)}), f32[32,2,64,64]{3,2,1,0:T(8,128)}) %all-gather.6.cloned.1.call-update) | async-done | bytes 1048592 | tf_op jit(solution)/shard_map/all_gather | solution.py:171
  40.5 1.5 fusion.19
  42.0 0.4 copy-done.7
  42.4 0.2 slice_bitcast_fusion
  42.7 0.6 maximum_maximum_fusion
  43.3 3.7 %reshape.49 = f32[32,2,64,2,64]{4,3,2,1,0:T(2,128)} reshape(f32[32,128,128]{2,1,0:T(8,128)S(1)} %maximum_maximum_fusion) | data formatting | bytes 4194304 | tf_op jit(solution)/shard_map/reshape | solution.py:180
  47.0 5.1 %fusion.4 = f32[2,32,32,64]{3,2,0,1:T(8,128)S(1)} fusion(f32[32,2,64,2,64]{4,3,2,1,0:T(2,128)} %reshape.49, f32[2,32,32,64,1]{3,1,2,0,4:T(8,128)S(1)} %convolution_bitcast_fusion), kind=kOutput, calls=%fused_computation.11 | convolution fusion | flops 201326592 | bytes 3145728 | tf_op jit(solution)/shard_map/rkpc,krcsd->skpd/dot_general | solution.py:131
  52.2 0.6 copy.49
  52.8 0.3 fusion.10
  53.1 0.1 broadcast_in_dim.4
  53.2 0.7 pad_maximum_fusion.2.coef_ref
  53.9 1.1 copy-done
  55.0 0.1 copy-done.4
  55.1 83.6 %middle.1 = (bf16[32,64,1024]{2,1,0:T(8,128)(2,1)}, bf16[32,64,1024]{2,1,0:T(8,128)(2,1)S(1)}, f32[32,64,128]{2,1,0:T(8,128)S(1)}, f32[256,64]{1,0:T(8,128)S(1)}, f32[256,64]{1,0:T(8,128)S(1)}) custom-call(bf16[32,64,1024]{2,1,0:T(8,128)(2,1)S(1)} %bitcast.69, bf16[32,64,1024]{2,1,0:T(8,128)(2,1)} %bitcast.75, ...), custom_call_target="tpu_custom_call" | custom-call | tf_op jit(solution)/shard_map/middle/pallas_call | solution.py:191
  138.7 1.9 copy-done.1
  140.7 1.3 slice_reduce_fusion
  142.1 0.1 reshape.54
  142.2 2.1 copy.53
  144.4 4.2 %fusion.14 = f32[32,2,64,2,64]{4,2,3,1,0:T(8,128)S(1)} fusion(f32[2,32,32,64,1]{3,1,2,0,4:T(8,128)S(1)} %convolution_bitcast_fusion, f32[2,32,32,64,1]{3,2,1,0,4:T(8,128)S(1)} %bitcast.72), kind=kOutput, calls=%fused_computation.24 | convolution fusion | flops 201326592 | bytes 3145728 | tf_op jit(solution)/shard_map/rkpc,skpd->krcsd/dot_general | solution.py:155
  148.6 5.8 %copy.60 = f32[32,2,64,2,64]{4,3,2,1,0:T(2,128)} copy(f32[32,2,64,2,64]{4,2,3,1,0:T(8,128)S(1)} %fusion.14) | data formatting | bytes 4194304 | tf_op jit(solution)/shard_map/rkpc,skpd->krcsd/dot_general | solution.py:155
  154.4 4.5 %reshape.52 = f32[32,128,128]{2,1,0:T(8,128)S(1)} reshape(f32[32,2,64,2,64]{4,3,2,1,0:T(2,128)} %copy.60) | data formatting | bytes 4194304 | tf_op jit(solution)/shard_map/reshape | solution.py:161
  158.9 0.6 fusion.13
  159.5 0.3 pad_maximum_fusion
  159.8 0.2 copy.61
  160.0 1.4 reshape.53
  161.4 2.3 %pad_maximum_fusion.1 = f32[8,292,128]{2,1,0:T(8,128)} fusion(f32[8,36,128]{2,1,0:T(8,128)S(1)} %reshape.54, f32[8,256,128]{2,1,0:T(8,128)} %reshape.53), kind=kLoop, calls=%fused_computation.13 | loop fusion | flops 299008 | bytes 2392064 | tf_op jit(solution)/shard_map/concatenate | solution.py:232
  163.7 3.6 %all-to-all-start = ((f32[8,292,128]{2,1,0:T(8,128)}), f32[8,292,128]{2,1,0:T(8,128)S(1)}, u32[]{:S(2)}, u32[]{:S(2)}) async-start(f32[8,292,128]{2,1,0:T(8,128)} %pad_maximum_fusion.1), calls=%async_computation | async-start | bytes 2424832 | tf_op jit(solution)/shard_map/all_to_all | solution.py:231
  167.3 7.7 %fusion.7 = f32[2,32,32,64]{3,2,0,1:T(8,128)S(1)} fusion(f32[32,2,64,2,64]{4,3,2,1,0:T(2,128)} %reshape.49, f32[2,32,32,64,1]{3,2,1,0,4:T(8,128)S(1)} %bitcast.73), kind=kOutput, calls=%fused_computation.12 | convolution fusion | flops 201326592 | bytes 3145728 | tf_op jit(solution)/shard_map/skpd,krcsd->rkpc/dot_general | solution.py:143
  175.1 0.6 copy.57
  175.8 0.3 fusion.11
  176.1 0.1 broadcast_in_dim.5
  176.2 0.7 pad_maximum_fusion.3.coef_ref
  176.9 1.1 copy-done.2
  177.9 0.1 copy-done.3
  178.1 8.3 %final.1 = bf16[32,64,1024]{2,1,0:T(8,128)(2,1)} custom-call(bf16[32,64,1024]{2,1,0:T(8,128)(2,1)S(1)} %copy-done.2, bf16[32,64,256]{2,1,0:T(8,128)(2,1)S(1)} %pad_maximum_fusion.3.coef_ref, bf16[192,1024]{1,0:T(8,128)(2,1)S(1)} %copy-done.3), custom_call_target="tpu_custom_call" | custom-call | tf_op jit(solution)/shard_map/final/pallas_call | solution.py:238
  186.5 17.5 %all-gather.2 = f32[4,292,128]{2,1,0:T(8,128)S(1)} all-gather(f32[1,292,128]{2,1,0:T(8,128)S(1)} %bitcast.78), channel_id=2, replica_groups=mesh['gy'=4,'gz'=8] {'gy'}, dimensions={0}, use_global_device_ids=true | all-gather | bytes 747520 | tf_op jit(solution)/shard_map/all_gather | solution.py:234
  204.0 9.6 %all-gather.3 = f32[8,36,128]{2,1,0:T(8,128)S(1)} all-gather(f32[1,36,128]{2,1,0:T(8,128)S(1)} %slice_bitcast_fusion.3), channel_id=3, replica_groups=mesh['gy'=4,'gz'=8] {'gz'}, dimensions={0}, use_global_device_ids=true | all-gather | bytes 165888 | tf_op jit(solution)/shard_map/all_gather | solution.py:236
  213.6 0.8 mul.30
  214.4 0.7 reshape.63
  215.1 0.1 reshape.67
  215.2 0.7 copy.64
  215.9 0.1 reshape.65
  216.0 0.7 copy.63
  (25 shorter events, 0.5 us)
Async XLA Ops:
  7.2 33.4 %all-gather.6.cloned.1.call-start = ((), (), s32[]{:S(2)}) async-start(), calls=%async_computation.1 | async-start | bytes 2359296 | tf_op jit(solution)/shard_map/all_gather | solution.py:171
  40.5 1.9 copy-start.7
  52.8 2.2 copy-start
  53.1 2.0 copy-start.4
  53.1 2.0 copy-start.5
  53.1 2.0 copy-start.6
  138.7 2.0 copy-start.1
  163.7 22.7 %all-to-all-start = ((f32[8,292,128]{2,1,0:T(8,128)}), f32[8,292,128]{2,1,0:T(8,128)S(1)}, u32[]{:S(2)}, u32[]{:S(2)}) async-start(f32[8,292,128]{2,1,0:T(8,128)} %pad_maximum_fusion.1), calls=%async_computation | async-start | bytes 2424832 | tf_op jit(solution)/shard_map/all_to_all | solution.py:231
  175.1 0.9 copy-start.8
  175.8 2.2 copy-start.2
  176.1 2.0 copy-start.3
Sparse Core Ops, SparseCore 0:
  9.9 30.5 all-gather.5

commit v2 on v1

--- a/solution.py
+++ b/solution.py
@@ -11,7 +11,7 @@
 MODES = 32
 
 
-CHUNK = 256
+CHUNK = 512
 GELU_SCALE = math.sqrt(2.0 / math.pi)
 GELU_CUBE = 0.044715
 

time: 224 us -> 201 us (0.90)
  Pallas kernels: 92 us -> 68.5 us
    pallas_call x1, Pallas kernels: 83.6 us -> 60.2 us  [local(): pl.pallas_call(middle_kernel, grid=(pencils // step,), in_specs=[per_penc...]
  transfers between devices with their start and end apart: 2 -> 2, of which waited for: 1 -> 1; matrix products, arithmetic and copies ran while one was open for 7% -> 8% of each run, Pallas kernels for 4% -> 4%
where the time goes in v2:
time: 201 us; the launch traced here: 200 us
  Pallas kernels  68.5 us (34%)
  local copies, waits for them, and re-layouts  30.2 us (15%)
  blocking collectives  27 us (13%)
  waiting for transfers between devices  26.3 us (13%)
  matrix products  21.4 us (11%)
  between operations  14.3 us (7%)
  other arithmetic  8.67 us (4%)
  starting transfers between devices  3.6 us (2%)
    pallas_call x1, Pallas kernels, local(): pl.pallas_call(middle_kernel, grid=(pencils // step,), in_specs=[per_penc...  60.2 us
    all_gather x1, waiting for transfers between devices, local(): gathered = lax.all_gather(spec_weight, 'gz', axis=0, tiled=True)  25.7 us
    all_gather x1, blocking collectives, local(): lax.all_gather(jnp.sum(shares, axis=0), 'gy', axis=0)  17.5 us
    all_gather x1, blocking collectives, local(): lax.all_gather(owned[spec_rows:], 'gz', axis=0).reshape(-1, channels)  9.48 us
    pallas_call x1, Pallas kernels, local(): pl.pallas_call(final_kernel, grid=(pencils // step,), in_specs=[per_penci...  8.33 us
    unnamed x24, local copies, waits for them, and re-layouts  8.04 us
    dot_general x1, matrix products, unmix_modes(): jnp.einsum('skpd,krcsd->rkpc', grads.reshape(halves, kept, pencils, chann...  7.74 us
    dot_general x1, local copies, waits for them, and re-layouts, mode_moment(): jnp.einsum('rkpc,skpd->krcsd', spectra.reshape(halves, kept, pencils, cha...  5.8 us
  transfers between devices with their start and end apart: 2, of which 1 were waited for; matrix products, arithmetic and copies ran while one was open for 8% of the time, Pallas kernels for 4%

profile of v2, /device:TPU:0, one launch (start us, length us, event | category | flops | bytes accessed | tf_op | source)
XLA Modules:
  0.0 200.1 jit_solution(6927710006375821705)
XLA Ops:
  7.2 0.7 all-gather.6.cloned.1.call-update
  7.9 0.8 copy.50
  8.7 0.9 copy.51
  9.6 0.9 copy.52.down_ref
  10.5 4.4 %convolution_bitcast_fusion = f32[2,32,32,64,1]{3,1,2,0,4:T(8,128)S(1)} fusion(bf16[2,32,1024,1]{2,1,3,0:T(8,128)(2,1)} %constant.20, bf16[32,64,1024,1]{2,1,0,3:T(8,128)(2,1)} %bitcast.68), kind=kOutput, calls=%fused_computation.10 | convolution fusion | flops 268435456 | bytes 4849664 | tf_op jit(solution)/shard_map/dot_general | solution.py:174
  14.9 25.7 %all-gather.6.cloned.1.call-done = f32[32,2,64,64]{3,2,1,0:T(8,128)} async-done(((f32[4,2,64,64]{3,2,1,0:T(8,128)}), f32[32,2,64,64]{3,2,1,0:T(8,128)}) %all-gather.6.cloned.1.call-update) | async-done | bytes 1048592 | tf_op jit(solution)/shard_map/all_gather | solution.py:171
  40.5 1.5 fusion.19
  42.0 0.4 copy-done.7
  42.4 0.2 slice_bitcast_fusion
  42.7 0.6 maximum_maximum_fusion
  43.3 3.7 %reshape.49 = f32[32,2,64,2,64]{4,3,2,1,0:T(2,128)} reshape(f32[32,128,128]{2,1,0:T(8,128)S(1)} %maximum_maximum_fusion) | data formatting | bytes 4194304 | tf_op jit(solution)/shard_map/reshape | solution.py:180
  47.0 5.1 %fusion.4 = f32[2,32,32,64]{3,2,0,1:T(8,128)S(1)} fusion(f32[32,2,64,2,64]{4,3,2,1,0:T(2,128)} %reshape.49, f32[2,32,32,64,1]{3,1,2,0,4:T(8,128)S(1)} %convolution_bitcast_fusion), kind=kOutput, calls=%fused_computation.11 | convolution fusion | flops 201326592 | bytes 3145728 | tf_op jit(solution)/shard_map/rkpc,krcsd->skpd/dot_general | solution.py:131
  52.2 0.6 copy.49
  52.8 0.3 fusion.10
  53.1 0.1 broadcast_in_dim.4
  53.2 0.7 pad_maximum_fusion.2.coef_ref
  53.9 1.1 copy-done
  55.0 0.1 copy-done.4
  55.1 60.2 %middle.1 = (bf16[32,64,1024]{2,1,0:T(8,128)(2,1)}, bf16[32,64,1024]{2,1,0:T(8,128)(2,1)S(1)}, f32[32,64,128]{2,1,0:T(8,128)S(1)}, f32[256,64]{1,0:T(8,128)S(1)}, f32[256,64]{1,0:T(8,128)S(1)}) custom-call(bf16[32,64,1024]{2,1,0:T(8,128)(2,1)S(1)} %bitcast.69, bf16[32,64,1024]{2,1,0:T(8,128)(2,1)} %bitcast.75, ...), custom_call_target="tpu_custom_call" | custom-call | tf_op jit(solution)/shard_map/middle/pallas_call | solution.py:191
  115.3 1.9 copy-done.1
  117.2 1.3 slice_reduce_fusion
  118.7 0.1 reshape.54
  118.8 2.1 %copy.53 = f32[64,32,64]{2,1,0:T(8,128)S(1)} copy(f32[64,32,64]{0,2,1:T(8,128)} %get-tuple-element.33) | data formatting | bytes 1048576 | tf_op jit(solution)/shard_map/transpose | solution.py:225
  121.0 4.2 %fusion.14 = f32[32,2,64,2,64]{4,2,3,1,0:T(8,128)S(1)} fusion(f32[2,32,32,64,1]{3,1,2,0,4:T(8,128)S(1)} %convolution_bitcast_fusion, f32[2,32,32,64,1]{3,2,1,0,4:T(8,128)S(1)} %bitcast.72), kind=kOutput, calls=%fused_computation.24 | convolution fusion | flops 201326592 | bytes 3145728 | tf_op jit(solution)/shard_map/rkpc,skpd->krcsd/dot_general | solution.py:155
  125.2 5.8 %copy.60 = f32[32,2,64,2,64]{4,3,2,1,0:T(2,128)} copy(f32[32,2,64,2,64]{4,2,3,1,0:T(8,128)S(1)} %fusion.14) | data formatting | bytes 4194304 | tf_op jit(solution)/shard_map/rkpc,skpd->krcsd/dot_general | solution.py:155
  130.9 4.5 %reshape.52 = f32[32,128,128]{2,1,0:T(8,128)S(1)} reshape(f32[32,2,64,2,64]{4,3,2,1,0:T(2,128)} %copy.60) | data formatting | bytes 4194304 | tf_op jit(solution)/shard_map/reshape | solution.py:161
  135.5 0.6 fusion.13
  136.1 0.3 pad_maximum_fusion
  136.3 0.2 copy.61
  136.6 1.4 reshape.53
  137.9 2.3 %pad_maximum_fusion.1 = f32[8,292,128]{2,1,0:T(8,128)} fusion(f32[8,36,128]{2,1,0:T(8,128)S(1)} %reshape.54, f32[8,256,128]{2,1,0:T(8,128)} %reshape.53), kind=kLoop, calls=%fused_computation.13 | loop fusion | flops 299008 | bytes 2392064 | tf_op jit(solution)/shard_map/concatenate | solution.py:232
  140.3 3.6 %all-to-all-start = ((f32[8,292,128]{2,1,0:T(8,128)}), f32[8,292,128]{2,1,0:T(8,128)S(1)}, u32[]{:S(2)}, u32[]{:S(2)}) async-start(f32[8,292,128]{2,1,0:T(8,128)} %pad_maximum_fusion.1), calls=%async_computation | async-start | bytes 2424832 | tf_op jit(solution)/shard_map/all_to_all | solution.py:231
  143.9 7.7 %fusion.7 = f32[2,32,32,64]{3,2,0,1:T(8,128)S(1)} fusion(f32[32,2,64,2,64]{4,3,2,1,0:T(2,128)} %reshape.49, f32[2,32,32,64,1]{3,2,1,0,4:T(8,128)S(1)} %bitcast.73), kind=kOutput, calls=%fused_computation.12 | convolution fusion | flops 201326592 | bytes 3145728 | tf_op jit(solution)/shard_map/skpd,krcsd->rkpc/dot_general | solution.py:143
  151.7 0.6 copy.57
  152.3 0.3 fusion.11
  152.6 0.1 broadcast_in_dim.5
  152.8 0.7 pad_maximum_fusion.3.coef_ref
  153.4 1.1 copy-done.2
  154.5 0.1 copy-done.3
  154.6 8.3 %final.1 = bf16[32,64,1024]{2,1,0:T(8,128)(2,1)} custom-call(bf16[32,64,1024]{2,1,0:T(8,128)(2,1)S(1)} %copy-done.2, bf16[32,64,256]{2,1,0:T(8,128)(2,1)S(1)} %pad_maximum_fusion.3.coef_ref, bf16[192,1024]{1,0:T(8,128)(2,1)S(1)} %copy-done.3), custom_call_target="tpu_custom_call" | custom-call | tf_op jit(solution)/shard_map/final/pallas_call | solution.py:238
  163.0 17.5 %all-gather.2 = f32[4,292,128]{2,1,0:T(8,128)S(1)} all-gather(f32[1,292,128]{2,1,0:T(8,128)S(1)} %bitcast.78), channel_id=2, replica_groups=mesh['gy'=4,'gz'=8] {'gy'}, dimensions={0}, use_global_device_ids=true | all-gather | bytes 747520 | tf_op jit(solution)/shard_map/all_gather | solution.py:234
  180.7 9.5 %all-gather.3 = f32[8,36,128]{2,1,0:T(8,128)S(1)} all-gather(f32[1,36,128]{2,1,0:T(8,128)S(1)} %slice_bitcast_fusion.3), channel_id=3, replica_groups=mesh['gy'=4,'gz'=8] {'gz'}, dimensions={0}, use_global_device_ids=true | all-gather | bytes 165888 | tf_op jit(solution)/shard_map/all_gather | solution.py:236
  190.2 0.8 mul.30
  191.0 0.7 reshape.63
  191.7 0.1 reshape.67
  191.8 0.7 copy.64
  192.5 0.1 reshape.65
  192.6 0.7 copy.63
  (25 shorter events, 0.5 us)
Async XLA Ops:
  7.2 33.4 %all-gather.6.cloned.1.call-start = ((), (), s32[]{:S(2)}) async-start(), calls=%async_computation.1 | async-start | bytes 2359296 | tf_op jit(solution)/shard_map/all_gather | solution.py:171
  40.5 1.9 copy-start.7
  52.8 2.2 %copy-start = (bf16[1024,4,8,64]{0,3,2,1:T(8,128)(2,1)S(1)}, bf16[1024,4,8,64]{0,3,2,1:T(8,128)(2,1)}, u32[]{:S(2)}) copy-start(bf16[1024,4,8,64]{0,3,2,1:T(8,128)(2,1)} %param.9) | copy-start | bytes 12582916
  53.1 2.0 %copy-start.4 = (bf16[192,1024]{1,0:T(8,128)(2,1)S(1)}, bf16[192,1024]{1,0:T(8,128)(2,1)}, u32[]{:S(2)}) copy-start(bf16[192,1024]{1,0:T(8,128)(2,1)} %constant.5.clone.table_ref) | copy-start | bytes 1179652
  53.1 2.0 %copy-start.5 = (bf16[64,256]{1,0:T(8,128)(2,1)S(1)}, bf16[64,256]{1,0:T(8,128)(2,1)}, u32[]{:S(2)}) copy-start(bf16[64,256]{1,0:T(8,128)(2,1)} %up_ref.1) | copy-start | bytes 98308
  53.1 2.0 %copy-start.6 = (bf16[256,64]{0,1:T(8,128)(2,1)S(1)}, bf16[256,64]{0,1:T(8,128)(2,1)}, u32[]{:S(2)}) copy-start(bf16[256,64]{0,1:T(8,128)(2,1)} %param.13) | copy-start | bytes 98308
  115.3 2.0 copy-start.1
  140.3 22.7 %all-to-all-start = ((f32[8,292,128]{2,1,0:T(8,128)}), f32[8,292,128]{2,1,0:T(8,128)S(1)}, u32[]{:S(2)}, u32[]{:S(2)}) async-start(f32[8,292,128]{2,1,0:T(8,128)} %pad_maximum_fusion.1), calls=%async_computation | async-start | bytes 2424832 | tf_op jit(solution)/shard_map/all_to_all | solution.py:231
  151.7 0.9 copy-start.8
  152.3 2.2 %copy-start.2 = (bf16[32,64,1024]{2,1,0:T(8,128)(2,1)S(1)}, bf16[32,64,1024]{2,1,0:T(8,128)(2,1)}, u32[]{:S(2)}) copy-start(bf16[32,64,1024]{2,1,0:T(8,128)(2,1)} %copy-done.1) | copy-start | bytes 12582916
  152.6 2.0 %copy-start.3 = (bf16[192,1024]{1,0:T(8,128)(2,1)S(1)}, bf16[192,1024]{1,0:T(8,128)(2,1)}, u32[]{:S(2)}) copy-start(bf16[192,1024]{1,0:T(8,128)(2,1)} %constant.16.clone.table_ref) | copy-start | bytes 1179652
Sparse Core Ops, SparseCore 0:
  9.9 30.5 all-gather.5
